TPU v7x, 32 devices: a whole 2x2x4 slice. The times are simulated.
32 devices in a mesh: island: 8 (over y, x, core), fsdp: 4 (over z).
Axes of the slice: x: 2, y: 2, z: 4, core: 2. Of those that a mesh axis runs over, the one named last changes fastest.
Arguments:
- tokens: bfloat16 [8, 1024, 12288], P('island', 'fsdp'), may hold values from -6 to 6
- targets: bfloat16 [8, 1024, 256], P('island', 'fsdp'), may hold values from -6 to 6
- loss_mask: int32 [8, 1024], P('island', 'fsdp'), may hold values 0 or 1
- norm_gain: float32 [12288], replicated, may hold values from 0.5 to 1.5
- params: float32 [8, 12288, 256], P('island', 'fsdp'), may hold values from -0.0546875 to 0.0546875
- moment_one: float32 [8, 12288, 256], P('island', 'fsdp'), may hold values from -0.12 to 0.12
- moment_two: float32 [8, 12288, 256], P('island', 'fsdp'), may hold values from 0.0001 to 0.002
- outer_delta: float32 [8, 12288, 128], P('island', 'fsdp'), may hold values from -6 to 6
- outer_momentum: float32 [12288, 128], P('fsdp'), may hold values from -6 to 6
Outputs:
- params_new: float32 [8, 12288, 256], P('island', 'fsdp')
- momentum_new: float32 [12288, 128], P('fsdp')
- outer_update: float32 [12288, 128], P('fsdp')
All inputs are finite; a program needn't handle non-finite values. No bound on the sum of `loss_mask` on one device may be relied on, other than what follows from the above.
Results may differ from a plain program's by a relative error of at most 0.0025.
Values may be sent and summed in bfloat16 or wider, within the bound.
A program may use at most 128 MiB of HBM per device.

v0:
```python
import jax
import jax.numpy as jnp
from jax import lax
from jax.sharding import PartitionSpec as P

ADAM_BETA_ONE = 0.9
ADAM_BETA_TWO = 0.95
ADAM_EPSILON = 1e-08
INNER_RATE = 0.005
WEIGHT_DECAY = 0.1
NORM_EPSILON = 1e-05
OUTER_RATE = 0.7
OUTER_MOMENTUM = 0.9
STEP_BASE = 1000


def adam_update(weights, first_moment, second_moment, gradient, count):
    first_moment = ADAM_BETA_ONE * first_moment + (1.0 - ADAM_BETA_ONE) * gradient
    second_moment = ADAM_BETA_TWO * second_moment + (1.0 - ADAM_BETA_TWO) * gradient * gradient
    first_hat = first_moment / (1.0 - ADAM_BETA_ONE**count)
    second_hat = second_moment / (1.0 - ADAM_BETA_TWO**count)
    weights = weights - INNER_RATE * (
        first_hat / (jnp.sqrt(second_hat) + ADAM_EPSILON) + WEIGHT_DECAY * weights
    )
    return (weights, first_moment, second_moment)


def per_device(
    tokens,
    targets,
    loss_mask,
    norm_gain,
    params,
    moment_one,
    moment_two,
    outer_delta,
    outer_momentum,
):
    fsdp_count = lax.axis_size("fsdp")
    token_island = tokens.shape[1] * fsdp_count
    weights = params[0]
    first_moment = moment_one[0]
    second_moment = moment_two[0]
    inputs_f = tokens[0].astype(jnp.float32)
    row_scale = lax.rsqrt(jnp.mean(inputs_f * inputs_f, axis=1) + NORM_EPSILON)
    scaled = (inputs_f * norm_gain).astype(jnp.bfloat16)
    keep_rows = loss_mask[0].astype(jnp.float32)
    goal_rows = targets[0].astype(jnp.float32)
    for inner_step in range(2):
        weights_bf = weights.astype(jnp.bfloat16)
        empty_rows = jnp.zeros((scaled.shape[0], weights_bf.shape[1]), jnp.float32)
        shard_rows = lax.all_gather(weights_bf, "fsdp", axis=0, tiled=True)
        columns = lax.slice_in_dim(scaled, 0, shard_rows.shape[0], axis=1)
        projected = empty_rows + jnp.dot(columns, shard_rows, preferred_element_type=jnp.float32)
        value_rows = row_scale[:, None] * projected
        residual_rows = (
            row_scale[:, None] * keep_rows[:, None] * (value_rows - goal_rows) / token_island
        ).astype(jnp.bfloat16)
        gradient = lax.psum_scatter(
            lax.dot_general(
                scaled, residual_rows, (((0,), (0,)), ((), ())), preferred_element_type=jnp.float32
            ).astype(jnp.bfloat16),
            "fsdp",
            scatter_dimension=0,
            tiled=True,
        ).astype(jnp.float32)
        weights, first_moment, second_moment = adam_update(
            weights, first_moment, second_moment, gradient, float(STEP_BASE + inner_step + 1)
        )
    island_count = lax.axis_size("island")
    summed = lax.psum(outer_delta[0], "island")
    outer_mean = summed / island_count
    momentum_new = OUTER_MOMENTUM * outer_momentum + outer_mean
    outer_update = OUTER_RATE * (outer_mean + OUTER_MOMENTUM * momentum_new)
    momentum_new, outer_update = (momentum_new, outer_update)
    return (weights[None], momentum_new, outer_update)


def solution(mesh):
    return jax.shard_map(
        per_device,
        mesh=mesh,
        in_specs=(
            P("island", "fsdp", None),
            P("island", "fsdp", None),
            P("island", "fsdp"),
            P(),
            P("island", "fsdp", None),
            P("island", "fsdp", None),
            P("island", "fsdp", None),
            P("island", "fsdp", None),
            P("fsdp", None),
        ),
        out_specs=(P("island", "fsdp", None), P("fsdp", None), P("fsdp", None)),
        check_vma=False,
    )
```

profile of v0, /device:TPU:0, one launch (start us, length us, event | category | flops | bytes accessed | tf_op | source)
XLA Modules:
  0.0 513.6 jit_solution(7365576714145901421)
XLA Ops:
  8.0 0.0 all-gather.3.cloned.1.call-start
  8.1 3.2 bitcast_convert_fusion
  11.2 0.0 all-gather.3.cloned.1.call-update
  11.3 0.0 reduce-scatter.3.cloned.1.call-start
  11.4 4.2 fusion.1
  15.5 113.9 %all-gather.3.cloned.1.call-done = bf16[12288,256]{1,0:T(8,128)(2,1)} async-done(((bf16[3072,256]{1,0:T(8,128)(2,1)}), bf16[12288,256]{1,0:T(8,128)(2,1)}) %all-gather.3.cloned.1.call-update) | async-done | bytes 6291472 | tf_op jit(solution)/shard_map/all_gather | solution.py:52
  129.5 6.4 %fusion.48 = bf16[256,256]{1,0:T(8,128)(2,1)S(1)} fusion(bf16[12288,256]{1,0:T(8,128)(2,1)} %all-gather.3.cloned.1.call-done, bf16[1,256,12288]{2,1,0:T(8,128)(2,1)} %param.9, f32[12288]{0:T(1024)S(1)} %copy-done.3, bf16[1,256,256]{2,1,0:T(8,128)(2,1)S(1)} %copy-done.2, f32[256]{0:T(256)S(1)} %get-tuple-element.6, f32[256]{0:T(256)S(1)} %get-tuple-element.5), kind=kOutput, calls=%fused_computation.39 | convolution fusion | flops 1620443136 | bytes 12896256 | tf_op jit(solution)/shard_map/dot_general | solution.py:54
  135.9 7.5 %convolution_convert_fusion.1 = bf16[12288,256]{1,0:T(8,128)(2,1)} fusion(bf16[256,256]{1,0:T(8,128)(2,1)S(1)} %fusion.48, bf16[1,256,12288]{2,1,0:T(8,128)(2,1)} %param.9, f32[12288]{0:T(1024)S(1)} %copy-done.3), kind=kOutput, calls=%fused_computation.3 | convolution fusion | flops 1623195648 | bytes 12763136 | tf_op jit(solution)/shard_map/dot_general | solution.py:60
  143.4 0.0 reduce-scatter.3.cloned.1.call-update
  143.4 0.0 all-gather.5.cloned.1.call-start
  143.5 109.1 %reduce-scatter.3.cloned.1.call-done = bf16[3072,256]{1,0:T(8,128)(2,1)} async-done(((bf16[12288,256]{1,0:T(8,128)(2,1)}), bf16[3072,256]{1,0:T(8,128)(2,1)}) %reduce-scatter.3.cloned.1.call-update) | async-done | bytes 1572880 | tf_op jit(solution)/shard_map/reduce_scatter | solution.py:59
  252.6 6.7 %fusion.52 = bf16[3072,256]{1,0:T(8,128)(2,1)} fusion(f32[1,3072,256]{2,1,0:T(8,128)} %param.15, bf16[3072,256]{1,0:T(8,128)(2,1)} %reduce-scatter.3.cloned.1.call-done, f32[1,3072,256]{2,1,0:T(8,128)} %param.14, f32[1,3072,256]{2,1,0:T(8,128)S(1)} %copy-done), kind=kLoop, calls=%fused_computation.42 | loop fusion | flops 11796480 | bytes 12582912 | tf_op jit(solution)/shard_map/convert_element_type | solution.py:50
  259.3 0.0 all-gather.5.cloned.1.call-update
  259.4 0.0 all-reduce.2.cloned.1.call-start
  259.4 0.5 all-reduce.2.cloned.1.call-update
  259.9 0.2 reduce-scatter.5.cloned.1.call-start
  260.2 115.2 %all-gather.5.cloned.1.call-done = bf16[12288,256]{1,0:T(8,128)(2,1)} async-done(((bf16[3072,256]{1,0:T(8,128)(2,1)}), bf16[12288,256]{1,0:T(8,128)(2,1)}) %all-gather.5.cloned.1.call-update) | async-done | bytes 6291472 | tf_op jit(solution)/shard_map/all_gather | solution.py:52
  375.4 6.4 %fusion.45 = bf16[256,256]{1,0:T(8,128)(2,1)S(1)} fusion(bf16[12288,256]{1,0:T(8,128)(2,1)} %all-gather.5.cloned.1.call-done, bf16[1,256,12288]{2,1,0:T(8,128)(2,1)} %param.9, f32[12288]{0:T(1024)S(1)} %copy-done.3, bf16[1,256,256]{2,1,0:T(8,128)(2,1)S(1)} %copy-done.2, f32[256]{0:T(256)S(1)} %get-tuple-element.6, f32[256]{0:T(256)S(1)} %get-tuple-element.5), kind=kOutput, calls=%fused_computation.38 | convolution fusion | flops 1620443136 | bytes 12896256 | tf_op jit(solution)/shard_map/dot_general | solution.py:54
  381.8 7.5 %convolution_convert_fusion = bf16[12288,256]{1,0:T(8,128)(2,1)} fusion(bf16[256,256]{1,0:T(8,128)(2,1)S(1)} %fusion.45, bf16[1,256,12288]{2,1,0:T(8,128)(2,1)} %param.9, f32[12288]{0:T(1024)S(1)} %copy-done.3), kind=kOutput, calls=%fused_computation.2 | convolution fusion | flops 1623195648 | bytes 12763136 | tf_op jit(solution)/shard_map/dot_general | solution.py:60
  389.3 0.0 reduce-scatter.5.cloned.1.call-update
  389.3 0.0 all-reduce.2.cloned.1.call-done
  389.4 3.9 add_multiply_fusion
  393.3 105.2 %reduce-scatter.5.cloned.1.call-done = bf16[3072,256]{1,0:T(8,128)(2,1)} async-done(((bf16[12288,256]{1,0:T(8,128)(2,1)}), bf16[3072,256]{1,0:T(8,128)(2,1)}) %reduce-scatter.5.cloned.1.call-update) | async-done | bytes 1572880 | tf_op jit(solution)/shard_map/reduce_scatter | solution.py:59
  498.5 8.0 %fusion.14 = f32[1,3072,256]{2,1,0:T(8,128)} fusion(bf16[3072,256]{1,0:T(8,128)(2,1)} %reduce-scatter.5.cloned.1.call-done, bf16[3072,256]{1,0:T(8,128)(2,1)} %reduce-scatter.3.cloned.1.call-done, f32[1,3072,256]{2,1,0:T(8,128)} %param.14, f32[1,3072,256]{2,1,0:T(8,128)} %param.15, f32[1,3072,256]{2,1,0:T(8,128)S(1)} %copy-done), kind=kLoop, calls=%fused_computation.18 | loop fusion | flops 22020096 | bytes 15728640 | tf_op jit(solution)/shard_map/broadcast_in_dim | solution.py:76
  (10 shorter events, 0.0 us)
Async XLA Ops:
  8.0 3.3 copy-start.1
  8.0 121.5 %all-gather.3.cloned.1.call-start = ((), (), s32[]{:S(2)}) async-start(), calls=%async_computation.2 | async-start | bytes 7864320 | tf_op jit(solution)/shard_map/all_gather | solution.py:52
  11.3 241.3 %reduce-scatter.3.cloned.1.call-start = ((), (), s32[]{:S(2)}) async-start(), calls=%async_computation.3 | async-start | bytes 7864320 | tf_op jit(solution)/shard_map/reduce_scatter | solution.py:59
  11.3 118.1 %copy-start.2 = (bf16[1,256,256]{2,1,0:T(8,128)(2,1)S(1)}, bf16[1,256,256]{2,1,0:T(8,128)(2,1)}, u32[]{:S(2)}) copy-start(bf16[1,256,256]{2,1,0:T(8,128)(2,1)} %param.10) | copy-start | bytes 393220
  11.3 118.1 %copy-start.3 = (f32[12288]{0:T(1024)S(1)}, f32[12288]{0:T(1024)}, u32[]{:S(2)}) copy-start(f32[12288]{0:T(1024)} %param.12) | copy-start | bytes 147460
  143.4 109.2 %copy-start = (f32[1,3072,256]{2,1,0:T(8,128)S(1)}, f32[1,3072,256]{2,1,0:T(8,128)}, u32[]{:S(2)}) copy-start(f32[1,3072,256]{2,1,0:T(8,128)} %param.13) | copy-start | bytes 9437188
  143.4 231.9 %all-gather.5.cloned.1.call-start = ((), (), s32[]{:S(2)}) async-start(), calls=%async_computation.4 | async-start | bytes 7864320 | tf_op jit(solution)/shard_map/all_gather | solution.py:52
  259.4 130.0 %all-reduce.2.cloned.1.call-start = ((), (), s32[]{:S(2)}) async-start(), calls=%async_computation.6 | async-start | bytes 3145728 | tf_op jit(solution)/shard_map/psum | solution.py:71
  259.9 238.5 %reduce-scatter.5.cloned.1.call-start = ((), (), s32[]{:S(2)}) async-start(), calls=%async_computation.5 | async-start | bytes 7864320 | tf_op jit(solution)/shard_map/reduce_scatter | solution.py:59
Sparse Core Ops, SparseCore 0:
  11.4 118.0 all-gather.2
  143.6 108.9 reduce-scatter.2
  259.5 115.8 all-gather.4
  389.5 108.9 reduce-scatter.4
Sparse Core Ops, SparseCore 1:
  263.1 58.6 all-reduce.1
where the time goes:
time: 514 us
  waiting for transfers between devices  444 us (86%)
  matrix products  27.9 us (5%)
  other arithmetic  26 us (5%)
  between operations  15.3 us (3%)
    all_gather x2, waiting for transfers between devices, per_device(): shard_rows = lax.all_gather(weights_bf, 'fsdp', axis=0, tiled=True)  229 us
    reduce_scatter x2, waiting for transfers between devices, per_device(): lax.psum_scatter(lax.dot_general(scaled, residual_rows, (((0,), (0,)), ((...  214 us
    dot_general x2, matrix products, per_device(): lax.dot_general(scaled, residual_rows, (((0,), (0,)), ((), ())), preferre...  15 us
    dot_general x2, matrix products, per_device(): jnp.dot(columns, shard_rows, preferred_element_type=jnp.float32)  12.8 us
  transfers between devices with their start and end apart: 5, of which 4 were waited for; matrix products, arithmetic and copies ran while one was open for 4% of the time, Pallas kernels for 0%

commit v1 on v0

v1 whole, which is shorter than its diff:
```python
import functools
import jax
import jax.numpy as jnp
from jax import lax
from jax.experimental import pallas as pl
from jax.experimental.pallas import tpu as pltpu
from jax.sharding import PartitionSpec as P

ADAM_BETA_ONE = 0.9
ADAM_BETA_TWO = 0.95
ADAM_EPSILON = 1e-08
INNER_RATE = 0.005
WEIGHT_DECAY = 0.1
NORM_EPSILON = 1e-05
OUTER_RATE = 0.7
OUTER_MOMENTUM = 0.9
STEP_BASE = 1000
MESH = pl.DeviceIdType.MESH
CHUNK = 128
BLOCK = 256


def adam_update(weights, first_moment, second_moment, gradient, count):
    first_moment = ADAM_BETA_ONE * first_moment + (1.0 - ADAM_BETA_ONE) * gradient
    second_moment = ADAM_BETA_TWO * second_moment + (1.0 - ADAM_BETA_TWO) * gradient * gradient
    first_hat = first_moment * (1.0 / (1.0 - ADAM_BETA_ONE**count))
    second_hat = second_moment * (1.0 / (1.0 - ADAM_BETA_TWO**count))
    weights = weights - INNER_RATE * (
        first_hat / (jnp.sqrt(second_hat) + ADAM_EPSILON) + WEIGHT_DECAY * weights
    )
    return (weights, first_moment, second_moment)


def inner_kernel(
    n,
    tokens,
    targets,
    mask,
    gain,
    params,
    moment_one,
    moment_two,
    out,
    xbuf,
    xt,
    tok,
    w,
    m1,
    m2,
    wbf,
    vsend,
    vrecv,
    vown,
    rbuf,
    scale,
    load_sem,
    out_sem,
    x_send,
    x_recv,
    v_send,
    v_recv,
    r_send,
    r_recv,
):
    me = lax.axis_index("fsdp")
    rows, width = tokens.shape
    feat = width // n
    chunks = rows // CHUNK
    blocks = feat // BLOCK
    island_tokens = rows * n

    def peer(k):
        return lax.rem(me + k, n)

    def source(k):
        return lax.rem(me + n - k, n)

    def own_rows(c):
        return pl.ds(pl.multiple_of(me * rows + c * CHUNK, CHUNK), CHUNK)

    def chunk_rows(c):
        return pl.ds(pl.multiple_of(c * CHUNK, CHUNK), CHUNK)

    def x_copy(k, c):
        to = peer(k)
        return pltpu.make_async_remote_copy(
            src_ref=tokens.at[chunk_rows(c), pl.ds(pl.multiple_of(to * feat, 128), feat)],
            dst_ref=xbuf.at[own_rows(c)],
            send_sem=x_send.at[k - 1, c],
            recv_sem=x_recv.at[k - 1, c],
            device_id={"fsdp": to},
            device_id_type=MESH,
        )

    def v_copy(step, k, c):
        return pltpu.make_async_remote_copy(
            src_ref=vsend.at[step, k - 1, chunk_rows(c)],
            dst_ref=vrecv.at[step, k - 1, chunk_rows(c)],
            send_sem=v_send.at[step, k - 1, c],
            recv_sem=v_recv.at[step, k - 1, c],
            device_id={"fsdp": source(k)},
            device_id_type=MESH,
        )

    def r_copy(step, k, c):
        return pltpu.make_async_remote_copy(
            src_ref=rbuf.at[step, own_rows(c)],
            dst_ref=rbuf.at[step, own_rows(c)],
            send_sem=r_send.at[step, k - 1, c],
            recv_sem=r_recv.at[step, k - 1, c],
            device_id={"fsdp": peer(k)},
            device_id_type=MESH,
        )

    def each(body):
        def run(k, carry):
            body(k)
            return carry

        lax.fori_loop(1, n, run, 0)

    barrier = pltpu.get_barrier_semaphore()
    each(
        lambda k: pl.semaphore_signal(
            barrier, inc=1, device_id={"fsdp": peer(k)}, device_id_type=MESH
        )
    )
    pl.semaphore_wait(barrier, n - 1)

    for c in range(chunks):
        each(lambda k: x_copy(k, c).start())

    load_own = pltpu.make_async_copy(
        tokens.at[:, pl.ds(pl.multiple_of(me * feat, 128), feat)],
        xbuf.at[pl.ds(pl.multiple_of(me * rows, CHUNK), rows)],
        load_sem.at[0],
    )
    load_w = pltpu.make_async_copy(params, w, load_sem.at[1])
    load_tok = pltpu.make_async_copy(tokens, tok, load_sem.at[2])
    load_m1 = pltpu.make_async_copy(moment_one, m1, load_sem.at[3])
    load_m2 = pltpu.make_async_copy(moment_two, m2, load_sem.at[4])
    for load in (load_w, load_own, load_tok, load_m1, load_m2):
        load.start()

    load_w.wait()

    def cast_block(b, carry):
        at = pl.ds(pl.multiple_of(b * BLOCK, BLOCK), BLOCK)
        wbf[at, :] = w[at, :].astype(jnp.bfloat16)
        return carry

    lax.fori_loop(0, blocks, cast_block, 0)

    def take_chunk(k, c):
        start = pl.multiple_of(source(k) * rows + c * CHUNK, CHUNK)
        at = pl.ds(start, CHUNK)

        def scale_block(b, carry):
            cols = pl.ds(pl.multiple_of(b * BLOCK, BLOCK), BLOCK)
            gains = gain[:, pl.ds(pl.multiple_of(me * feat + b * BLOCK, BLOCK), BLOCK)]
            scaled = xbuf[at, cols].astype(jnp.float32) * gains
            xbuf[at, cols] = scaled.astype(jnp.bfloat16)
            xt[cols, at] = scaled.T.astype(jnp.bfloat16)
            return carry

        lax.fori_loop(0, blocks, scale_block, 0)
        return jnp.dot(xbuf[at, :], wbf[...], preferred_element_type=jnp.float32)

    def residual(step, c):
        at = chunk_rows(c)
        each(lambda k: v_copy(step, k, c).wait_recv())
        total = vown[step, at, :]
        for k in range(1, n):
            total = total + vrecv[step, k - 1, at, :].astype(jnp.float32)
        row_scale = scale[at, :]
        keep = mask[at, :].astype(jnp.float32)
        goal = targets[at, :].astype(jnp.float32)
        result = row_scale * keep * (row_scale * total - goal) / island_tokens
        rbuf[step, own_rows(c), :] = result.astype(jnp.bfloat16)
        each(lambda k: r_copy(step, k, c).start())

    load_own.wait()
    for c in range(chunks):
        vown[0, chunk_rows(c), :] = take_chunk(0, c)

    load_tok.wait()

    def square(b, total):
        part = tok[:, pl.ds(pl.multiple_of(b * 128, 128), 128)].astype(jnp.float32)
        return total + part * part

    squares = lax.fori_loop(0, width // 128, square, jnp.zeros((rows, 128), jnp.float32))
    mean = jnp.sum(squares, axis=1, keepdims=True) / width
    scale[...] = lax.rsqrt(mean + NORM_EPSILON)
    load_m1.wait()
    load_m2.wait()

    for c in range(chunks):

        def arrive(k):
            x_copy(k, c).wait_recv()
            vsend[0, k - 1, chunk_rows(c), :] = take_chunk(k, c).astype(jnp.bfloat16)
            v_copy(0, k, c).start()

        each(arrive)
        if c:
            residual(0, c - 1)
    residual(0, chunks - 1)

    def update(step):
        for c in range(chunks):
            each(lambda k: r_copy(step, k, c).wait_recv())

        def update_block(b, carry):
            at = pl.ds(pl.multiple_of(b * BLOCK, BLOCK), BLOCK)
            gradient = jnp.dot(xt[at, :], rbuf[step], preferred_element_type=jnp.float32)
            new_w, new_m1, new_m2 = adam_update(
                w[at, :], m1[at, :], m2[at, :], gradient, float(STEP_BASE + step + 1)
            )
            w[at, :] = new_w
            if step == 0:
                m1[at, :] = new_m1
                m2[at, :] = new_m2
                wbf[at, :] = new_w.astype(jnp.bfloat16)
            else:
                pltpu.make_async_copy(w.at[at], out.at[at], out_sem.at[b]).start()
            return carry

        lax.fori_loop(0, blocks, update_block, 0)

    update(0)

    def partial(k, c):
        at = pl.ds(pl.multiple_of(source(k) * rows + c * CHUNK, CHUNK), CHUNK)
        return jnp.dot(xbuf[at, :], wbf[...], preferred_element_type=jnp.float32)

    for c in range(chunks):

        def send(k):
            vsend[1, k - 1, chunk_rows(c), :] = partial(k, c).astype(jnp.bfloat16)
            v_copy(1, k, c).start()

        each(send)
    for c in range(chunks):
        vown[1, chunk_rows(c), :] = partial(0, c)
    for c in range(chunks):
        residual(1, c)
    update(1)

    def finish(b, carry):
        at = pl.ds(pl.multiple_of(b * BLOCK, BLOCK), BLOCK)
        pltpu.make_async_copy(w.at[at], out.at[at], out_sem.at[b]).wait()
        return carry

    lax.fori_loop(0, blocks, finish, 0)
    for c in range(chunks):

        def drain(k):
            x_copy(k, c).wait_send()
            for step in range(2):
                v_copy(step, k, c).wait_send()
                r_copy(step, k, c).wait_send()

        each(drain)


def inner_steps(n, tokens, targets, mask, gain, params, moment_one, moment_two):
    rows, width = tokens.shape
    feat, columns = params.shape
    chunks = rows // CHUNK
    vmem = pl.BlockSpec(memory_space=pltpu.VMEM)
    hbm = pl.BlockSpec(memory_space=pl.ANY)
    dma = pltpu.SemaphoreType.DMA
    bf16, f32 = jnp.bfloat16, jnp.float32
    return pl.pallas_call(
        functools.partial(inner_kernel, n),
        out_shape=jax.ShapeDtypeStruct((feat, columns), f32),
        in_specs=[hbm, vmem, vmem, vmem, hbm, hbm, hbm],
        out_specs=hbm,
        scratch_shapes=[
            pltpu.VMEM((rows * n, feat), bf16),
            pltpu.VMEM((feat, rows * n), bf16),
            pltpu.VMEM((rows, width), bf16),
            pltpu.VMEM((feat, columns), f32),
            pltpu.VMEM((feat, columns), f32),
            pltpu.VMEM((feat, columns), f32),
            pltpu.VMEM((feat, columns), bf16),
            pltpu.VMEM((2, n - 1, rows, columns), bf16),
            pltpu.VMEM((2, n - 1, rows, columns), bf16),
            pltpu.VMEM((2, rows, columns), f32),
            pltpu.VMEM((2, rows * n, columns), bf16),
            pltpu.VMEM((rows, 1), f32),
            dma((5,)),
            dma((feat // BLOCK,)),
            dma((n - 1, chunks)),
            dma((n - 1, chunks)),
            dma((2, n - 1, chunks)),
            dma((2, n - 1, chunks)),
            dma((2, n - 1, chunks)),
            dma((2, n - 1, chunks)),
        ],
        compiler_params=pltpu.CompilerParams(
            collective_id=0, has_side_effects=True, vmem_limit_bytes=56 * 2**20
        ),
        cost_estimate=pl.CostEstimate(
            flops=8 * rows * n * feat * columns,
            bytes_accessed=4 * rows * width + 16 * feat * columns,
            transcendentals=4 * feat * columns,
        ),
    )(tokens, targets, mask, gain, params, moment_one, moment_two)


def per_device(
    tokens,
    targets,
    loss_mask,
    norm_gain,
    params,
    moment_one,
    moment_two,
    outer_delta,
    outer_momentum,
):
    n = lax.axis_size("fsdp")
    island_count = lax.axis_size("island")
    summed = lax.psum(outer_delta[0], "island")
    weights = inner_steps(
        n,
        tokens[0],
        targets[0],
        loss_mask[0][:, None],
        norm_gain[None, :],
        params[0],
        moment_one[0],
        moment_two[0],
    )
    outer_mean = summed / island_count
    momentum_new = OUTER_MOMENTUM * outer_momentum + outer_mean
    outer_update = OUTER_RATE * (outer_mean + OUTER_MOMENTUM * momentum_new)
    return (weights[None], momentum_new, outer_update)


def solution(mesh):
    return jax.shard_map(
        per_device,
        mesh=mesh,
        in_specs=(
            P("island", "fsdp", None),
            P("island", "fsdp", None),
            P("island", "fsdp"),
            P(),
            P("island", "fsdp", None),
            P("island", "fsdp", None),
            P("island", "fsdp", None),
            P("island", "fsdp", None),
            P("fsdp", None),
        ),
        out_specs=(P("island", "fsdp", None), P("fsdp", None), P("fsdp", None)),
        check_vma=False,
    )
```

time: 514 us -> 220 us (0.43)
  waiting for transfers between devices: 444 us -> 0.7 us
  Pallas kernels: 0 us -> 199 us
  matrix products: 27.9 us -> 0 us
  other arithmetic: 26 us -> 3.59 us
    all_gather x2 -> x0, waiting for transfers between devices: 229 us -> none  [per_device(): shard_rows = lax.all_gather(weights_bf, 'fsdp', axis=0, tiled=True)]
    reduce_scatter x2 -> x0, waiting for transfers between devices: 214 us -> none  [per_device(): lax.psum_scatter(lax.dot_general(scaled, residual_rows, (((0,), (0,)), ((...]
    pallas_call x0 -> x1, Pallas kernels: none -> 199 us  [inner_steps(): pl.pallas_call(functools.partial(inner_kernel, n), out_shape=jax.ShapeDty...]
    dot_general x4 -> x0, matrix products: 27.9 us -> none  [the longest x2 15 us: per_device(): lax.dot_general(scaled, residual_rows, (((0,), (0,)), ((), ())), preferre...]
    convert_element_type x3 -> x0, other arithmetic: 9.94 us -> none  [the longest x2 9.94 us: per_device(): weights_bf = weights.astype(jnp.bfloat16)]
    broadcast_in_dim x1 -> x0, other arithmetic: 8 us -> none  [per_device(): return (weights[None], momentum_new, outer_update)]
  transfers between devices with their start and end apart: 5 -> 1, of which waited for: 4 -> 0; matrix products, arithmetic and copies ran while one was open for 4% -> 0% of each run, Pallas kernels for 0% -> 90%
where the time goes in v1:
time: 220 us; the launch traced here: 219 us
  Pallas kernels  199 us (90%)
  between operations  14.1 us (6%)
  other arithmetic  3.59 us (2%)
  local copies, waits for them, and re-layouts  2.48 us (1%)
    pallas_call x1, Pallas kernels, inner_steps(): pl.pallas_call(functools.partial(inner_kernel, n), out_shape=jax.ShapeDty...  199 us
  transfers between devices with their start and end apart: 1, of which 0 were waited for; matrix products, arithmetic and copies ran while one was open for 0% of the time, Pallas kernels for 90%

profile of v1, /device:TPU:0, one launch (start us, length us, event | category | flops | bytes accessed | tf_op | source)
XLA Modules:
  0.0 219.4 jit_solution(3973338133084011054)
XLA Ops:
  7.2 0.0 copy-start.2
  7.2 0.0 all-reduce.2.cloned.1.call-start
  7.2 0.7 all-reduce.2.cloned.1.call-update
  7.9 0.0 copy-done.2
  7.9 0.8 copy.12.mask
  8.7 0.0 copy-start.1
  8.7 198.6 %shard_map.112 = f32[3072,256]{1,0:T(8,128)} custom-call(bf16[256,12288]{1,0:T(8,128)(2,1)} %bitcast.12, bf16[256,256]{1,0:T(8,128)(2,1)} %bitcast.16, s32[256,1]{1,0:T(8,128)} %copy.12.mask, f32[1,12288]{1,0:T(1,128)} %bitcast.17, f32[3072,256]{1,0:T(8,128)} %bitcast.13, f32[3072,256]{1,0:T(8,128)} %bitcast.14, f32[3072,256]{1,0:T(8,128)} %bitcast.15), custom_call_target="tpu_custom_call" | custom-call | flops 6442450944 | bytes 25165824 | tf_op jit(solution)/shard_map/pallas_call | solution.py:275
  207.3 0.0 all-reduce.2.cloned.1.call-done
  207.3 0.0 copy-done.1
  207.3 0.0 copy-start
  207.3 3.6 %add_multiply_fusion = (f32[3072,128]{1,0:T(8,128)}, f32[3072,128]{1,0:T(8,128)}) fusion(f32[3072,128]{1,0:T(8,128)} %all-reduce.2.cloned.1.call-done, f32[3072,128]{1,0:T(8,128)S(1)} %copy-done.1), kind=kLoop, calls=%fused_computation | loop fusion | flops 2359296 | bytes 6291456 | tf_op jit(solution)/shard_map/mul | solution.py:339
  210.9 0.0 copy-done
  210.9 1.7 copy.16
Async XLA Ops:
  7.2 0.7 copy-start.2
  7.2 200.1 %all-reduce.2.cloned.1.call-start = ((), (), s32[]{:S(2)}) async-start(), calls=%async_computation | async-start | bytes 3145728 | tf_op jit(solution)/shard_map/psum | solution.py:326
  8.7 198.6 %copy-start.1 = (f32[3072,128]{1,0:T(8,128)S(1)}, f32[3072,128]{1,0:T(8,128)}, u32[]{:S(2)}) copy-start(f32[3072,128]{1,0:T(8,128)} %param.17) | copy-start | bytes 4718596
  207.3 3.6 %copy-start = (f32[3072,256]{1,0:T(8,128)S(1)}, f32[3072,256]{1,0:T(8,128)}, u32[]{:S(2)}) copy-start(f32[3072,256]{1,0:T(8,128)} %shard_map.112) | copy-start | bytes 9437188
Sparse Core Ops, SparseCore 0:
  11.3 61.6 all-reduce.1

commit v2 on v1

--- a/solution.py
+++ b/solution.py
@@ -18,6 +18,8 @@
 MESH = pl.DeviceIdType.MESH
 CHUNK = 128
 BLOCK = 256
+UNITS = 4
+WINDOW = 3
 
 
 def adam_update(weights, first_moment, second_moment, gradient, count):
@@ -33,6 +35,7 @@
 
 def inner_kernel(
     n,
+    m,
     tokens,
     targets,
     mask,
@@ -40,7 +43,11 @@
     params,
     moment_one,
     moment_two,
+    delta,
+    outer_momentum,
     out,
+    momentum_out,
+    update_out,
     xbuf,
     xt,
     tok,
@@ -48,11 +55,16 @@
     m1,
     m2,
     wbf,
+    vacc,
     vsend,
     vrecv,
     vown,
     rbuf,
     scale,
+    keep,
+    dbuf,
+    total_buf,
+    outer_buf,
     load_sem,
     out_sem,
     x_send,
@@ -61,13 +73,20 @@
     v_recv,
     r_send,
     r_recv,
+    d_send,
+    d_recv,
+    a_send,
+    a_recv,
 ):
     me = lax.axis_index("fsdp")
+    isle = lax.axis_index("island")
     rows, width = tokens.shape
     feat = width // n
     chunks = rows // CHUNK
     blocks = feat // BLOCK
+    unit = feat // UNITS
     island_tokens = rows * n
+    slab = delta.shape[0] // m
 
     def peer(k):
         return lax.rem(me + k, n)
@@ -81,13 +100,18 @@
     def chunk_rows(c):
         return pl.ds(pl.multiple_of(c * CHUNK, CHUNK), CHUNK)
 
-    def x_copy(k, c):
+    def slab_rows(i):
+        return pl.ds(pl.multiple_of(i * slab, 8), slab)
+
+    def x_copy(k, u):
+        c, q = u // UNITS, u % UNITS
         to = peer(k)
+        cols = pl.ds(pl.multiple_of(to * feat + q * unit, 128), unit)
         return pltpu.make_async_remote_copy(
-            src_ref=tokens.at[chunk_rows(c), pl.ds(pl.multiple_of(to * feat, 128), feat)],
-            dst_ref=xbuf.at[own_rows(c)],
-            send_sem=x_send.at[k - 1, c],
-            recv_sem=x_recv.at[k - 1, c],
+            src_ref=tokens.at[chunk_rows(c), cols],
+            dst_ref=xbuf.at[own_rows(c), pl.ds(q * unit, unit)],
+            send_sem=x_send.at[k - 1, u],
+            recv_sem=x_recv.at[k - 1, u],
             device_id={"fsdp": to},
             device_id_type=MESH,
         )
@@ -112,12 +136,33 @@
             device_id_type=MESH,
         )
 
-    def each(body):
+    def d_copy(j):
+        to = lax.rem(isle + j, m)
+        return pltpu.make_async_remote_copy(
+            src_ref=delta.at[slab_rows(to)],
+            dst_ref=dbuf.at[j],
+            send_sem=d_send.at[j - 1],
+            recv_sem=d_recv.at[j - 1],
+            device_id={"island": to},
+            device_id_type=MESH,
+        )
+
+    def a_copy(j):
+        return pltpu.make_async_remote_copy(
+            src_ref=total_buf.at[slab_rows(isle)],
+            dst_ref=total_buf.at[slab_rows(isle)],
+            send_sem=a_send.at[j - 1],
+            recv_sem=a_recv.at[j - 1],
+            device_id={"island": lax.rem(isle + j, m)},
+            device_id_type=MESH,
+        )
+
+    def each(body, count=n):
         def run(k, carry):
             body(k)
             return carry
 
-        lax.fori_loop(1, n, run, 0)
+        lax.fori_loop(1, count, run, 0)
 
     barrier = pltpu.get_barrier_semaphore()
     each(
@@ -125,10 +170,17 @@
             barrier, inc=1, device_id={"fsdp": peer(k)}, device_id_type=MESH
         )
     )
-    pl.semaphore_wait(barrier, n - 1)
-
-    for c in range(chunks):
-        each(lambda k: x_copy(k, c).start())
+    each(
+        lambda j: pl.semaphore_signal(
+            barrier, inc=1, device_id={"island": lax.rem(isle + j, m)}, device_id_type=MESH
+        ),
+        m,
+    )
+    pl.semaphore_wait(barrier, n + m - 2)
+
+    last_unit = chunks * UNITS
+    for u in range(min(WINDOW, last_unit)):
+        each(lambda k: x_copy(k, u).start())
 
     load_own = pltpu.make_async_copy(
         tokens.at[:, pl.ds(pl.multiple_of(me * feat, 128), feat)],
@@ -139,7 +191,12 @@
     load_tok = pltpu.make_async_copy(tokens, tok, load_sem.at[2])
     load_m1 = pltpu.make_async_copy(moment_one, m1, load_sem.at[3])
     load_m2 = pltpu.make_async_copy(moment_two, m2, load_sem.at[4])
-    for load in (load_w, load_own, load_tok, load_m1, load_m2):
+    load_d = pltpu.make_async_copy(delta.at[slab_rows(isle)], dbuf.at[0], load_sem.at[5])
+    load_outer = pltpu.make_async_copy(outer_momentum, outer_buf, load_sem.at[6])
+    load_w.start()
+    load_own.start()
+    each(lambda j: d_copy(j).start(), m)
+    for load in (load_d, load_tok, load_m1, load_m2, load_outer):
         load.start()
 
     load_w.wait()
@@ -151,20 +208,19 @@
 
     lax.fori_loop(0, blocks, cast_block, 0)
 
-    def take_chunk(k, c):
-        start = pl.multiple_of(source(k) * rows + c * CHUNK, CHUNK)
-        at = pl.ds(start, CHUNK)
-
-        def scale_block(b, carry):
-            cols = pl.ds(pl.multiple_of(b * BLOCK, BLOCK), BLOCK)
-            gains = gain[:, pl.ds(pl.multiple_of(me * feat + b * BLOCK, BLOCK), BLOCK)]
+    def take_unit(k, u):
+        c, q = u // UNITS, u % UNITS
+        at = pl.ds(pl.multiple_of(source(k) * rows + c * CHUNK, CHUNK), CHUNK)
+        for b in range(unit // 128):
+            first = q * unit + b * 128
+            cols = pl.ds(first, 128)
+            gains = gain[:, pl.ds(pl.multiple_of(me * feat + first, 128), 128)]
             scaled = xbuf[at, cols].astype(jnp.float32) * gains
             xbuf[at, cols] = scaled.astype(jnp.bfloat16)
             xt[cols, at] = scaled.T.astype(jnp.bfloat16)
-            return carry
-
-        lax.fori_loop(0, blocks, scale_block, 0)
-        return jnp.dot(xbuf[at, :], wbf[...], preferred_element_type=jnp.float32)
+        cols = pl.ds(q * unit, unit)
+        part = jnp.dot(xbuf[at, cols], wbf[cols, :], preferred_element_type=jnp.float32)
+        return part if q == 0 else vacc[k] + part
 
     def residual(step, c):
         at = chunk_rows(c)
@@ -173,15 +229,24 @@
         for k in range(1, n):
             total = total + vrecv[step, k - 1, at, :].astype(jnp.float32)
         row_scale = scale[at, :]
-        keep = mask[at, :].astype(jnp.float32)
         goal = targets[at, :].astype(jnp.float32)
-        result = row_scale * keep * (row_scale * total - goal) / island_tokens
+        result = row_scale * keep[at, :] * (row_scale * total - goal) / island_tokens
         rbuf[step, own_rows(c), :] = result.astype(jnp.bfloat16)
         each(lambda k: r_copy(step, k, c).start())
 
     load_own.wait()
-    for c in range(chunks):
-        vown[0, chunk_rows(c), :] = take_chunk(0, c)
+    for u in range(last_unit):
+        if u % UNITS == UNITS - 1:
+            vown[0, chunk_rows(u // UNITS), :] = take_unit(0, u)
+        else:
+            vacc[0] = take_unit(0, u)
+
+    load_d.wait()
+    each(lambda j: d_copy(j).wait_recv(), m)
+    total_buf[slab_rows(isle), :] = lax.fori_loop(
+        1, m, lambda j, total: total + dbuf[j], dbuf[0]
+    )
+    each(lambda j: a_copy(j).start(), m)
 
     load_tok.wait()
 
@@ -192,18 +257,52 @@
     squares = lax.fori_loop(0, width // 128, square, jnp.zeros((rows, 128), jnp.float32))
     mean = jnp.sum(squares, axis=1, keepdims=True) / width
     scale[...] = lax.rsqrt(mean + NORM_EPSILON)
+    keep_row = jnp.broadcast_to(mask[...].astype(jnp.float32), (128, rows))
+    keep[...] = keep_row.T[:, :1]
     load_m1.wait()
     load_m2.wait()
-
-    for c in range(chunks):
+    load_outer.wait()
+
+    def outer_copies():
+        return (
+            pltpu.make_async_copy(outer_buf, momentum_out, load_sem.at[7]),
+            pltpu.make_async_copy(total_buf, update_out, load_sem.at[8]),
+        )
+
+    def outer_step():
+        each(lambda j: a_copy(j).wait_recv(), m)
+        each(lambda j: a_copy(j).wait_send(), m)
+
+        def outer_block(b, carry):
+            at = pl.ds(pl.multiple_of(b * BLOCK, BLOCK), BLOCK)
+            outer_mean = total_buf[at, :] / m
+            momentum_new = OUTER_MOMENTUM * outer_buf[at, :] + outer_mean
+            outer_buf[at, :] = momentum_new
+            total_buf[at, :] = OUTER_RATE * (outer_mean + OUTER_MOMENTUM * momentum_new)
+            return carry
+
+        lax.fori_loop(0, blocks, outer_block, 0)
+        for copy in outer_copies():
+            copy.start()
+
+    for u in range(last_unit):
+        c, q = u // UNITS, u % UNITS
 
         def arrive(k):
-            x_copy(k, c).wait_recv()
-            vsend[0, k - 1, chunk_rows(c), :] = take_chunk(k, c).astype(jnp.bfloat16)
-            v_copy(0, k, c).start()
+            x_copy(k, u).wait_recv()
+            if u + WINDOW < last_unit:
+                x_copy(k, u + WINDOW).start()
+            part = take_unit(k, u)
+            if q == UNITS - 1:
+                vsend[0, k - 1, chunk_rows(c), :] = part.astype(jnp.bfloat16)
+                v_copy(0, k, c).start()
+            else:
+                vacc[k] = part
 
         each(arrive)
-        if c:
+        if u == UNITS - 1:
+            outer_step()
+        if c and q == UNITS // 2:
             residual(0, c - 1)
     residual(0, chunks - 1)
 
@@ -230,19 +329,17 @@
 
     update(0)
 
-    def partial(k, c):
-        at = pl.ds(pl.multiple_of(source(k) * rows + c * CHUNK, CHUNK), CHUNK)
+    def partial(k):
+        at = pl.ds(pl.multiple_of(source(k) * rows, CHUNK), rows)
         return jnp.dot(xbuf[at, :], wbf[...], preferred_element_type=jnp.float32)
 
-    for c in range(chunks):
-
-        def send(k):
-            vsend[1, k - 1, chunk_rows(c), :] = partial(k, c).astype(jnp.bfloat16)
+    def send(k):
+        vsend[1, k - 1] = partial(k).astype(jnp.bfloat16)
+        for c in range(chunks):
             v_copy(1, k, c).start()
 
-        each(send)
-    for c in range(chunks):
-        vown[1, chunk_rows(c), :] = partial(0, c)
+    each(send)
+    vown[1] = partial(0)
     for c in range(chunks):
         residual(1, c)
     update(1)
@@ -253,30 +350,39 @@
         return carry
 
     lax.fori_loop(0, blocks, finish, 0)
-    for c in range(chunks):
-
-        def drain(k):
-            x_copy(k, c).wait_send()
+    for copy in outer_copies():
+        copy.wait()
+
+    def drain(k):
+        for u in range(last_unit):
+            x_copy(k, u).wait_send()
+        for c in range(chunks):
             for step in range(2):
                 v_copy(step, k, c).wait_send()
                 r_copy(step, k, c).wait_send()
 
-        each(drain)
-
-
-def inner_steps(n, tokens, targets, mask, gain, params, moment_one, moment_two):
+    each(drain)
+    each(lambda j: d_copy(j).wait_send(), m)
+
+
+def train(n, m, tokens, targets, mask, gain, params, moment_one, moment_two, delta, momentum):
     rows, width = tokens.shape
     feat, columns = params.shape
     chunks = rows // CHUNK
+    slab = delta.shape[0] // m
     vmem = pl.BlockSpec(memory_space=pltpu.VMEM)
     hbm = pl.BlockSpec(memory_space=pl.ANY)
     dma = pltpu.SemaphoreType.DMA
     bf16, f32 = jnp.bfloat16, jnp.float32
     return pl.pallas_call(
-        functools.partial(inner_kernel, n),
-        out_shape=jax.ShapeDtypeStruct((feat, columns), f32),
-        in_specs=[hbm, vmem, vmem, vmem, hbm, hbm, hbm],
-        out_specs=hbm,
+        functools.partial(inner_kernel, n, m),
+        out_shape=(
+            jax.ShapeDtypeStruct((feat, columns), f32),
+            jax.ShapeDtypeStruct(momentum.shape, f32),
+            jax.ShapeDtypeStruct(momentum.shape, f32),
+        ),
+        in_specs=[hbm, vmem, vmem, vmem, hbm, hbm, hbm, hbm, hbm],
+        out_specs=(hbm, hbm, hbm),
         scratch_shapes=[
             pltpu.VMEM((rows * n, feat), bf16),
             pltpu.VMEM((feat, rows * n), bf16),
@@ -285,19 +391,28 @@
             pltpu.VMEM((feat, columns), f32),
             pltpu.VMEM((feat, columns), f32),
             pltpu.VMEM((feat, columns), bf16),
+            pltpu.VMEM((n, CHUNK, columns), f32),
             pltpu.VMEM((2, n - 1, rows, columns), bf16),
             pltpu.VMEM((2, n - 1, rows, columns), bf16),
             pltpu.VMEM((2, rows, columns), f32),
             pltpu.VMEM((2, rows * n, columns), bf16),
             pltpu.VMEM((rows, 1), f32),
-            dma((5,)),
+            pltpu.VMEM((rows, 1), f32),
+            pltpu.VMEM((m, slab, delta.shape[1]), f32),
+            pltpu.VMEM(delta.shape, f32),
+            pltpu.VMEM(delta.shape, f32),
+            dma((9,)),
             dma((feat // BLOCK,)),
-            dma((n - 1, chunks)),
-            dma((n - 1, chunks)),
+            dma((n - 1, chunks * UNITS)),
+            dma((n - 1, chunks * UNITS)),
             dma((2, n - 1, chunks)),
             dma((2, n - 1, chunks)),
             dma((2, n - 1, chunks)),
             dma((2, n - 1, chunks)),
+            dma((m - 1,)),
+            dma((m - 1,)),
+            dma((m - 1,)),
+            dma((m - 1,)),
         ],
         compiler_params=pltpu.CompilerParams(
             collective_id=0, has_side_effects=True, vmem_limit_bytes=56 * 2**20
@@ -307,7 +422,7 @@
             bytes_accessed=4 * rows * width + 16 * feat * columns,
             transcendentals=4 * feat * columns,
         ),
-    )(tokens, targets, mask, gain, params, moment_one, moment_two)
+    )(tokens, targets, mask, gain, params, moment_one, moment_two, delta, momentum)
 
 
 def per_device(
@@ -321,22 +436,19 @@
     outer_delta,
     outer_momentum,
 ):
-    n = lax.axis_size("fsdp")
-    island_count = lax.axis_size("island")
-    summed = lax.psum(outer_delta[0], "island")
-    weights = inner_steps(
-        n,
+    weights, momentum_new, outer_update = train(
+        lax.axis_size("fsdp"),
+        lax.axis_size("island"),
         tokens[0],
         targets[0],
-        loss_mask[0][:, None],
+        loss_mask,
         norm_gain[None, :],
         params[0],
         moment_one[0],
         moment_two[0],
-    )
-    outer_mean = summed / island_count
-    momentum_new = OUTER_MOMENTUM * outer_momentum + outer_mean
-    outer_update = OUTER_RATE * (outer_mean + OUTER_MOMENTUM * momentum_new)
+        outer_delta[0],
+        outer_momentum,
+    )
     return (weights[None], momentum_new, outer_update)
 
 

time: 220 us -> 209 us (0.950)
  between operations: 14.1 us -> 0.65 us
  local copies, waits for them, and re-layouts: 2.48 us -> 7 us
  other arithmetic: 3.59 us -> 0 us
    unnamed x7, local copies, waits for them, and re-layouts: 1.68 us -> 7 us
    mul x1 -> x0, other arithmetic: 3.59 us -> none  [per_device(): outer_update = OUTER_RATE * (outer_mean + OUTER_MOMENTUM * momentum_new)]
    pallas_call x1, Pallas kernels: 199 us -> 201 us  [train(): pl.pallas_call(functools.partial(inner_kernel, n, m), out_shape=(jax.Shap...]
  transfers between devices with their start and end apart: 1 -> 0, of which waited for: 0 -> 0; matrix products, arithmetic and copies ran while one was open for 0% -> 0% of each run, Pallas kernels for 90% -> 0%
where the time goes in v2:
time: 209 us
  Pallas kernels  201 us (96%)
  local copies, waits for them, and re-layouts  7 us (3%)
    pallas_call x1, Pallas kernels, train(): pl.pallas_call(functools.partial(inner_kernel, n, m), out_shape=(jax.Shap...  201 us
    unnamed x7, local copies, waits for them, and re-layouts  7 us

profile of v2, /device:TPU:0, one launch (start us, length us, event | category | flops | bytes accessed | tf_op | source)
XLA Modules:
  0.0 208.8 jit_solution(313898838277344913)
XLA Ops:
  0.6 201.2 %shard_map.112 = (f32[3072,256]{1,0:T(8,128)}, f32[3072,128]{1,0:T(8,128)}, f32[3072,128]{1,0:T(8,128)}) custom-call(bf16[256,12288]{1,0:T(8,128)(2,1)} %bitcast.9, bf16[256,256]{1,0:T(8,128)(2,1)} %bitcast.14, s32[1,256]{1,0:T(1,128)} %mask.1, f32[1,12288]{1,0:T(1,128)} %bitcast.15, f32[3072,256]{1,0:T(8,128)} %bitcast.10, f32[3072,256]{1,0:T(8,128)} %bitcast.11, ...), custom_call_target="tpu_custom_call" | custom-call | flops 6442450944 | bytes 25165824 | tf_op jit(solution)/shard_map/pallas_call | solution.py:377
  201.8 0.0 copy-start.1
  201.8 3.9 %copy.15 = f32[1,3072,256]{2,1,0:T(8,128)} copy(f32[1,3072,256]{2,1,0:T(8,128)} %bitcast.8) | data formatting | bytes 6291456
  205.7 0.0 copy-done.1
  205.7 0.0 copy-start
  205.7 1.1 copy.16
  206.9 0.8 copy-done
  207.7 1.1 copy.17
Async XLA Ops:
  201.8 3.9 %copy-start.1 = (f32[3072,128]{1,0:T(8,128)S(1)}, f32[3072,128]{1,0:T(8,128)}, u32[]{:S(2)}) copy-start(f32[3072,128]{1,0:T(8,128)} %get-tuple-element.13) | copy-start | bytes 4718596
  205.7 2.0 copy-start

commit v3 on v2

--- a/solution.py
+++ b/solution.py
@@ -16,9 +16,9 @@
 OUTER_MOMENTUM = 0.9
 STEP_BASE = 1000
 MESH = pl.DeviceIdType.MESH
-CHUNK = 128
+CHUNK = 64
 BLOCK = 256
-UNITS = 4
+UNITS = 2
 WINDOW = 3
 
 
@@ -66,7 +66,6 @@
     total_buf,
     outer_buf,
     load_sem,
-    out_sem,
     x_send,
     x_recv,
     v_send,
@@ -217,10 +216,18 @@
             gains = gain[:, pl.ds(pl.multiple_of(me * feat + first, 128), 128)]
             scaled = xbuf[at, cols].astype(jnp.float32) * gains
             xbuf[at, cols] = scaled.astype(jnp.bfloat16)
-            xt[cols, at] = scaled.T.astype(jnp.bfloat16)
         cols = pl.ds(q * unit, unit)
         part = jnp.dot(xbuf[at, cols], wbf[cols, :], preferred_element_type=jnp.float32)
         return part if q == 0 else vacc[k] + part
+
+    def turn_unit(k, u):
+        c, q = u // UNITS, u % UNITS
+        if c % 2:
+            start = source(k) * rows + (c - 1) * CHUNK
+            at = pl.ds(pl.multiple_of(start, 2 * CHUNK), 2 * CHUNK)
+            for b in range(unit // 128):
+                cols = pl.ds(q * unit + b * 128, 128)
+                xt[cols, at] = xbuf[at, cols].astype(jnp.float32).T.astype(jnp.bfloat16)
 
     def residual(step, c):
         at = chunk_rows(c)
@@ -240,6 +247,7 @@
             vown[0, chunk_rows(u // UNITS), :] = take_unit(0, u)
         else:
             vacc[0] = take_unit(0, u)
+        turn_unit(0, u)
 
     load_d.wait()
     each(lambda j: d_copy(j).wait_recv(), m)
@@ -263,12 +271,6 @@
     load_m2.wait()
     load_outer.wait()
 
-    def outer_copies():
-        return (
-            pltpu.make_async_copy(outer_buf, momentum_out, load_sem.at[7]),
-            pltpu.make_async_copy(total_buf, update_out, load_sem.at[8]),
-        )
-
     def outer_step():
         each(lambda j: a_copy(j).wait_recv(), m)
         each(lambda j: a_copy(j).wait_send(), m)
@@ -277,13 +279,11 @@
             at = pl.ds(pl.multiple_of(b * BLOCK, BLOCK), BLOCK)
             outer_mean = total_buf[at, :] / m
             momentum_new = OUTER_MOMENTUM * outer_buf[at, :] + outer_mean
-            outer_buf[at, :] = momentum_new
-            total_buf[at, :] = OUTER_RATE * (outer_mean + OUTER_MOMENTUM * momentum_new)
+            momentum_out[at, :] = momentum_new
+            update_out[at, :] = OUTER_RATE * (outer_mean + OUTER_MOMENTUM * momentum_new)
             return carry
 
         lax.fori_loop(0, blocks, outer_block, 0)
-        for copy in outer_copies():
-            copy.start()
 
     for u in range(last_unit):
         c, q = u // UNITS, u % UNITS
@@ -298,11 +298,12 @@
                 v_copy(0, k, c).start()
             else:
                 vacc[k] = part
+            turn_unit(k, u)
 
         each(arrive)
         if u == UNITS - 1:
             outer_step()
-        if c and q == UNITS // 2:
+        if c and q == (0 if c == chunks - 1 else UNITS - 1):
             residual(0, c - 1)
     residual(0, chunks - 1)
 
@@ -316,13 +317,13 @@
             new_w, new_m1, new_m2 = adam_update(
                 w[at, :], m1[at, :], m2[at, :], gradient, float(STEP_BASE + step + 1)
             )
-            w[at, :] = new_w
             if step == 0:
+                w[at, :] = new_w
                 m1[at, :] = new_m1
                 m2[at, :] = new_m2
                 wbf[at, :] = new_w.astype(jnp.bfloat16)
             else:
-                pltpu.make_async_copy(w.at[at], out.at[at], out_sem.at[b]).start()
+                out[at, :] = new_w
             return carry
 
         lax.fori_loop(0, blocks, update_block, 0)
@@ -343,15 +344,6 @@
     for c in range(chunks):
         residual(1, c)
     update(1)
-
-    def finish(b, carry):
-        at = pl.ds(pl.multiple_of(b * BLOCK, BLOCK), BLOCK)
-        pltpu.make_async_copy(w.at[at], out.at[at], out_sem.at[b]).wait()
-        return carry
-
-    lax.fori_loop(0, blocks, finish, 0)
-    for copy in outer_copies():
-        copy.wait()
 
     def drain(k):
         for u in range(last_unit):
@@ -377,12 +369,12 @@
     return pl.pallas_call(
         functools.partial(inner_kernel, n, m),
         out_shape=(
-            jax.ShapeDtypeStruct((feat, columns), f32),
-            jax.ShapeDtypeStruct(momentum.shape, f32),
-            jax.ShapeDtypeStruct(momentum.shape, f32),
+            pltpu.VMEM((feat, columns), f32),
+            pltpu.VMEM(momentum.shape, f32),
+            pltpu.VMEM(momentum.shape, f32),
         ),
         in_specs=[hbm, vmem, vmem, vmem, hbm, hbm, hbm, hbm, hbm],
-        out_specs=(hbm, hbm, hbm),
+        out_specs=(vmem, vmem, vmem),
         scratch_shapes=[
             pltpu.VMEM((rows * n, feat), bf16),
             pltpu.VMEM((feat, rows * n), bf16),
@@ -401,8 +393,7 @@
             pltpu.VMEM((m, slab, delta.shape[1]), f32),
             pltpu.VMEM(delta.shape, f32),
             pltpu.VMEM(delta.shape, f32),
-            dma((9,)),
-            dma((feat // BLOCK,)),
+            dma((7,)),
             dma((n - 1, chunks * UNITS)),
             dma((n - 1, chunks * UNITS)),
             dma((2, n - 1, chunks)),
@@ -415,7 +406,7 @@
             dma((m - 1,)),
         ],
         compiler_params=pltpu.CompilerParams(
-            collective_id=0, has_side_effects=True, vmem_limit_bytes=56 * 2**20
+            collective_id=0, has_side_effects=True, vmem_limit_bytes=54 * 2**20
         ),
         cost_estimate=pl.CostEstimate(
             flops=8 * rows * n * feat * columns,

time: 209 us -> 208 us (level)
  local copies, waits for them, and re-layouts: 7 us -> 3.95 us
  Pallas kernels: 201 us -> 204 us
    unnamed x7 -> x3, local copies, waits for them, and re-layouts: 7 us -> 3.95 us
    pallas_call x1, Pallas kernels: 201 us -> 204 us  [train(): pl.pallas_call(functools.partial(inner_kernel, n, m), out_shape=(pltpu.VM...]
where the time goes in v3:
time: 208 us
  Pallas kernels  204 us (98%)
  local copies, waits for them, and re-layouts  3.95 us (2%)
    pallas_call x1, Pallas kernels, train(): pl.pallas_call(functools.partial(inner_kernel, n, m), out_shape=(pltpu.VM...  204 us

profile of v3, /device:TPU:0, one launch (start us, length us, event | category | flops | bytes accessed | tf_op | source)
XLA Modules:
  0.0 208.3 jit_solution(654693772179831147)
XLA Ops:
  0.6 203.7 %shard_map.112 = (f32[3072,256]{1,0:T(8,128)S(1)}, f32[3072,128]{1,0:T(8,128)S(1)}, f32[3072,128]{1,0:T(8,128)S(1)}) custom-call(bf16[256,12288]{1,0:T(8,128)(2,1)} %bitcast.9, bf16[256,256]{1,0:T(8,128)(2,1)} %bitcast.14, s32[1,256]{1,0:T(1,128)} %mask.1, f32[1,12288]{1,0:T(1,128)} %bitcast.15, f32[3072,256]{1,0:T(8,128)} %bitcast.10, ...), custom_call_target="tpu_custom_call" | custom-call | flops 6442450944 | bytes 25165824 | tf_op jit(solution)/shard_map/pallas_call | solution.py:369
  204.3 1.7 copy.15
  206.0 1.1 copy.16
  207.1 1.1 copy.17

commit v4 on v3

--- a/solution.py
+++ b/solution.py
@@ -28,7 +28,7 @@
     first_hat = first_moment * (1.0 / (1.0 - ADAM_BETA_ONE**count))
     second_hat = second_moment * (1.0 / (1.0 - ADAM_BETA_TWO**count))
     weights = weights - INNER_RATE * (
-        first_hat / (jnp.sqrt(second_hat) + ADAM_EPSILON) + WEIGHT_DECAY * weights
+        first_hat / (second_hat * lax.rsqrt(second_hat) + ADAM_EPSILON) + WEIGHT_DECAY * weights
     )
     return (weights, first_moment, second_moment)
 
@@ -59,6 +59,8 @@
     vsend,
     vrecv,
     vown,
+    vcross,
+    gbuf,
     rbuf,
     scale,
     keep,
@@ -135,6 +137,34 @@
             device_id_type=MESH,
         )
 
+    paired = n == 4
+    partner = me + 1 - 2 * lax.rem(me, 2)
+    across = lax.rem(me + 2, 4)
+    k_partner = 3 - 2 * lax.rem(me, 2)
+    k_far = 4 - k_partner
+
+    def pair_v(step, j, c):
+        return pltpu.make_async_remote_copy(
+            src_ref=vsend.at[step, j, chunk_rows(c)],
+            dst_ref=vrecv.at[step, j, chunk_rows(c)],
+            send_sem=v_send.at[step, j, c],
+            recv_sem=v_recv.at[step, j, c],
+            device_id={"fsdp": across if j == 2 else partner},
+            device_id_type=MESH,
+        )
+
+    def pair_r(step, j, c):
+        owner = across if j == 2 else me
+        at = pl.ds(pl.multiple_of(owner * rows + c * CHUNK, CHUNK), CHUNK)
+        return pltpu.make_async_remote_copy(
+            src_ref=rbuf.at[step, at],
+            dst_ref=rbuf.at[step, at],
+            send_sem=r_send.at[step, j, c],
+            recv_sem=r_recv.at[step, j, c],
+            device_id={"fsdp": across if j == 1 else partner},
+            device_id_type=MESH,
+        )
+
     def d_copy(j):
         to = lax.rem(isle + j, m)
         return pltpu.make_async_remote_copy(
@@ -229,17 +259,39 @@
                 cols = pl.ds(q * unit + b * 128, 128)
                 xt[cols, at] = xbuf[at, cols].astype(jnp.float32).T.astype(jnp.bfloat16)
 
+    def combine(step, c):
+        if paired:
+            at = chunk_rows(c)
+            pair_v(step, 1, c).wait_recv()
+            both = vcross[step, at, :] + vrecv[step, 1, at, :].astype(jnp.float32)
+            vsend[step, 2, at, :] = both.astype(jnp.bfloat16)
+            pair_v(step, 2, c).start()
+
     def residual(step, c):
         at = chunk_rows(c)
-        each(lambda k: v_copy(step, k, c).wait_recv())
         total = vown[step, at, :]
-        for k in range(1, n):
-            total = total + vrecv[step, k - 1, at, :].astype(jnp.float32)
+        if paired:
+            for j in (0, 2):
+                pair_v(step, j, c).wait_recv()
+                total = total + vrecv[step, j, at, :].astype(jnp.float32)
+        else:
+            each(lambda k: v_copy(step, k, c).wait_recv())
+            for k in range(1, n):
+                total = total + vrecv[step, k - 1, at, :].astype(jnp.float32)
         row_scale = scale[at, :]
         goal = targets[at, :].astype(jnp.float32)
         result = row_scale * keep[at, :] * (row_scale * total - goal) / island_tokens
         rbuf[step, own_rows(c), :] = result.astype(jnp.bfloat16)
-        each(lambda k: r_copy(step, k, c).start())
+        if paired:
+            pair_r(step, 1, c).start()
+            pair_r(step, 0, c).start()
+        else:
+            each(lambda k: r_copy(step, k, c).start())
+
+    def forward(step, c):
+        if paired:
+            pair_r(step, 1, c).wait_recv()
+            pair_r(step, 2, c).start()
 
     load_own.wait()
     for u in range(last_unit):
@@ -292,31 +344,54 @@
             x_copy(k, u).wait_recv()
             if u + WINDOW < last_unit:
                 x_copy(k, u + WINDOW).start()
-            part = take_unit(k, u)
-            if q == UNITS - 1:
-                vsend[0, k - 1, chunk_rows(c), :] = part.astype(jnp.bfloat16)
+            vacc[k] = take_unit(k, u)
+            if not paired and q == UNITS - 1:
+                vsend[0, k - 1, chunk_rows(c), :] = vacc[k].astype(jnp.bfloat16)
                 v_copy(0, k, c).start()
-            else:
-                vacc[k] = part
-            turn_unit(k, u)
+            if u < last_unit - 1:
+                turn_unit(k, u)
 
         each(arrive)
+        if paired and q == UNITS - 1:
+            at = chunk_rows(c)
+            for j, k in ((1, k_far), (0, k_partner)):
+                vsend[0, j, at, :] = vacc[k].astype(jnp.bfloat16)
+                pair_v(0, j, c).start()
+            vcross[0, at, :] = vacc[2]
         if u == UNITS - 1:
             outer_step()
-        if c and q == (0 if c == chunks - 1 else UNITS - 1):
-            residual(0, c - 1)
-    residual(0, chunks - 1)
+        for stage, act in enumerate((combine, residual, forward)):
+            done = u - UNITS - stage
+            if done >= 0 and done % UNITS == 0:
+                act(0, done // UNITS)
+    for stage, act in enumerate((combine, residual, forward)):
+        for c in range(chunks):
+            if UNITS * c + UNITS + stage >= last_unit:
+                act(0, c)
+        if stage == 0:
+            each(lambda k: turn_unit(k, last_unit - 1))
 
     def update(step):
         for c in range(chunks):
-            each(lambda k: r_copy(step, k, c).wait_recv())
+            if paired:
+                pair_r(step, 0, c).wait_recv()
+                pair_r(step, 2, c).wait_recv()
+            else:
+                each(lambda k: r_copy(step, k, c).wait_recv())
+
+        def gradient(b):
+            at = pl.ds(pl.multiple_of(b * BLOCK, BLOCK), BLOCK)
+            return jnp.dot(xt[at, :], rbuf[step], preferred_element_type=jnp.float32)
+
+        gbuf[0] = gradient(0)
 
         def update_block(b, carry):
             at = pl.ds(pl.multiple_of(b * BLOCK, BLOCK), BLOCK)
-            gradient = jnp.dot(xt[at, :], rbuf[step], preferred_element_type=jnp.float32)
             new_w, new_m1, new_m2 = adam_update(
-                w[at, :], m1[at, :], m2[at, :], gradient, float(STEP_BASE + step + 1)
+                w[at, :], m1[at, :], m2[at, :], gbuf[b % 2], float(STEP_BASE + step + 1)
             )
+            following = gradient(jnp.minimum(b + 1, blocks - 1))
+            gbuf[(b + 1) % 2] = following
             if step == 0:
                 w[at, :] = new_w
                 m1[at, :] = new_m1
@@ -339,10 +414,19 @@
         for c in range(chunks):
             v_copy(1, k, c).start()
 
-    each(send)
+    if paired:
+        for j, k in ((1, k_far), (0, k_partner)):
+            vsend[1, j] = partial(k).astype(jnp.bfloat16)
+            for c in range(chunks):
+                pair_v(1, j, c).start()
+        vcross[1] = partial(2)
+    else:
+        each(send)
     vown[1] = partial(0)
-    for c in range(chunks):
-        residual(1, c)
+    for t in range(chunks + 2):
+        for stage, act in enumerate((combine, residual, forward)):
+            if 0 <= t - stage < chunks:
+                act(1, t - stage)
     update(1)
 
     def drain(k):
@@ -350,10 +434,17 @@
             x_copy(k, u).wait_send()
         for c in range(chunks):
             for step in range(2):
-                v_copy(step, k, c).wait_send()
-                r_copy(step, k, c).wait_send()
+                if not paired:
+                    v_copy(step, k, c).wait_send()
+                    r_copy(step, k, c).wait_send()
 
     each(drain)
+    if paired:
+        for step in range(2):
+            for c in range(chunks):
+                for j in range(3):
+                    pair_v(step, j, c).wait_send()
+                    pair_r(step, j, c).wait_send()
     each(lambda j: d_copy(j).wait_send(), m)
 
 
@@ -387,6 +478,8 @@
             pltpu.VMEM((2, n - 1, rows, columns), bf16),
             pltpu.VMEM((2, n - 1, rows, columns), bf16),
             pltpu.VMEM((2, rows, columns), f32),
+            pltpu.VMEM((2, rows, columns), f32),
+            pltpu.VMEM((2, BLOCK, columns), f32),
             pltpu.VMEM((2, rows * n, columns), bf16),
             pltpu.VMEM((rows, 1), f32),
             pltpu.VMEM((rows, 1), f32),

time: 208 us -> 203 us (0.976)
  Pallas kernels: 204 us -> 198 us
    pallas_call x1, Pallas kernels: 204 us -> 198 us  [train(): pl.pallas_call(functools.partial(inner_kernel, n, m), out_shape=(pltpu.VM...]
where the time goes in v4:
time: 203 us
  Pallas kernels  198 us (98%)
  local copies, waits for them, and re-layouts  3.95 us (2%)
    pallas_call x1, Pallas kernels, train(): pl.pallas_call(functools.partial(inner_kernel, n, m), out_shape=(pltpu.VM...  198 us

profile of v4, /device:TPU:0, one launch (start us, length us, event | category | flops | bytes accessed | tf_op | source)
XLA Modules:
  0.0 202.8 jit_solution(5945921868496689382)
XLA Ops:
  0.6 198.2 %shard_map.112 = (f32[3072,256]{1,0:T(8,128)S(1)}, f32[3072,128]{1,0:T(8,128)S(1)}, f32[3072,128]{1,0:T(8,128)S(1)}) custom-call(bf16[256,12288]{1,0:T(8,128)(2,1)} %bitcast.9, bf16[256,256]{1,0:T(8,128)(2,1)} %bitcast.14, s32[1,256]{1,0:T(1,128)} %mask.1, f32[1,12288]{1,0:T(1,128)} %bitcast.15, f32[3072,256]{1,0:T(8,128)} %bitcast.10, ...), custom_call_target="tpu_custom_call" | custom-call | flops 6442450944 | bytes 25165824 | tf_op jit(solution)/shard_map/pallas_call | solution.py:460
  198.9 1.7 copy.15
  200.6 1.1 copy.16
  201.7 1.1 copy.17

commit v5 on v4

--- a/solution.py
+++ b/solution.py
@@ -25,10 +25,10 @@
 def adam_update(weights, first_moment, second_moment, gradient, count):
     first_moment = ADAM_BETA_ONE * first_moment + (1.0 - ADAM_BETA_ONE) * gradient
     second_moment = ADAM_BETA_TWO * second_moment + (1.0 - ADAM_BETA_TWO) * gradient * gradient
-    first_hat = first_moment * (1.0 / (1.0 - ADAM_BETA_ONE**count))
+    rate_one = INNER_RATE / (1.0 - ADAM_BETA_ONE**count)
     second_hat = second_moment * (1.0 / (1.0 - ADAM_BETA_TWO**count))
-    weights = weights - INNER_RATE * (
-        first_hat / (second_hat * lax.rsqrt(second_hat) + ADAM_EPSILON) + WEIGHT_DECAY * weights
+    weights = (1.0 - INNER_RATE * WEIGHT_DECAY) * weights - rate_one * first_moment / (
+        second_hat * lax.rsqrt(second_hat) + ADAM_EPSILON
     )
     return (weights, first_moment, second_moment)
 
@@ -95,11 +95,14 @@
     def source(k):
         return lax.rem(me + n - k, n)
 
-    def own_rows(c):
-        return pl.ds(pl.multiple_of(me * rows + c * CHUNK, CHUNK), CHUNK)
-
-    def chunk_rows(c):
-        return pl.ds(pl.multiple_of(c * CHUNK, CHUNK), CHUNK)
+    def size(step):
+        return CHUNK * (step + 1)
+
+    def own_rows(c, step=0):
+        return pl.ds(pl.multiple_of(me * rows + c * size(step), size(step)), size(step))
+
+    def chunk_rows(c, step=0):
+        return pl.ds(pl.multiple_of(c * size(step), size(step)), size(step))
 
     def slab_rows(i):
         return pl.ds(pl.multiple_of(i * slab, 8), slab)
@@ -119,8 +122,8 @@
 
     def v_copy(step, k, c):
         return pltpu.make_async_remote_copy(
-            src_ref=vsend.at[step, k - 1, chunk_rows(c)],
-            dst_ref=vrecv.at[step, k - 1, chunk_rows(c)],
+            src_ref=vsend.at[step, k - 1, chunk_rows(c, step)],
+            dst_ref=vrecv.at[step, k - 1, chunk_rows(c, step)],
             send_sem=v_send.at[step, k - 1, c],
             recv_sem=v_recv.at[step, k - 1, c],
             device_id={"fsdp": source(k)},
@@ -129,8 +132,8 @@
 
     def r_copy(step, k, c):
         return pltpu.make_async_remote_copy(
-            src_ref=rbuf.at[step, own_rows(c)],
-            dst_ref=rbuf.at[step, own_rows(c)],
+            src_ref=rbuf.at[step, own_rows(c, step)],
+            dst_ref=rbuf.at[step, own_rows(c, step)],
             send_sem=r_send.at[step, k - 1, c],
             recv_sem=r_recv.at[step, k - 1, c],
             device_id={"fsdp": peer(k)},
@@ -145,8 +148,8 @@
 
     def pair_v(step, j, c):
         return pltpu.make_async_remote_copy(
-            src_ref=vsend.at[step, j, chunk_rows(c)],
-            dst_ref=vrecv.at[step, j, chunk_rows(c)],
+            src_ref=vsend.at[step, j, chunk_rows(c, step)],
+            dst_ref=vrecv.at[step, j, chunk_rows(c, step)],
             send_sem=v_send.at[step, j, c],
             recv_sem=v_recv.at[step, j, c],
             device_id={"fsdp": across if j == 2 else partner},
@@ -155,7 +158,8 @@
 
     def pair_r(step, j, c):
         owner = across if j == 2 else me
-        at = pl.ds(pl.multiple_of(owner * rows + c * CHUNK, CHUNK), CHUNK)
+        first = pl.multiple_of(owner * rows + c * size(step), size(step))
+        at = pl.ds(first, size(step))
         return pltpu.make_async_remote_copy(
             src_ref=rbuf.at[step, at],
             dst_ref=rbuf.at[step, at],
@@ -261,14 +265,14 @@
 
     def combine(step, c):
         if paired:
-            at = chunk_rows(c)
+            at = chunk_rows(c, step)
             pair_v(step, 1, c).wait_recv()
             both = vcross[step, at, :] + vrecv[step, 1, at, :].astype(jnp.float32)
             vsend[step, 2, at, :] = both.astype(jnp.bfloat16)
             pair_v(step, 2, c).start()
 
     def residual(step, c):
-        at = chunk_rows(c)
+        at = chunk_rows(c, step)
         total = vown[step, at, :]
         if paired:
             for j in (0, 2):
@@ -281,7 +285,7 @@
         row_scale = scale[at, :]
         goal = targets[at, :].astype(jnp.float32)
         result = row_scale * keep[at, :] * (row_scale * total - goal) / island_tokens
-        rbuf[step, own_rows(c), :] = result.astype(jnp.bfloat16)
+        rbuf[step, own_rows(c, step), :] = result.astype(jnp.bfloat16)
         if paired:
             pair_r(step, 1, c).start()
             pair_r(step, 0, c).start()
@@ -372,7 +376,7 @@
             each(lambda k: turn_unit(k, last_unit - 1))
 
     def update(step):
-        for c in range(chunks):
+        for c in range(chunks // (step + 1)):
             if paired:
                 pair_r(step, 0, c).wait_recv()
                 pair_r(step, 2, c).wait_recv()
@@ -411,29 +415,29 @@
 
     def send(k):
         vsend[1, k - 1] = partial(k).astype(jnp.bfloat16)
-        for c in range(chunks):
+        for c in range(chunks // 2):
             v_copy(1, k, c).start()
 
     if paired:
         for j, k in ((1, k_far), (0, k_partner)):
             vsend[1, j] = partial(k).astype(jnp.bfloat16)
-            for c in range(chunks):
+            for c in range(chunks // 2):
                 pair_v(1, j, c).start()
         vcross[1] = partial(2)
     else:
         each(send)
     vown[1] = partial(0)
-    for t in range(chunks + 2):
+    for t in range(chunks // 2 + 2):
         for stage, act in enumerate((combine, residual, forward)):
-            if 0 <= t - stage < chunks:
+            if 0 <= t - stage < chunks // 2:
                 act(1, t - stage)
     update(1)
 
     def drain(k):
         for u in range(last_unit):
             x_copy(k, u).wait_send()
-        for c in range(chunks):
-            for step in range(2):
+        for step in range(2):
+            for c in range(chunks // (step + 1)):
                 if not paired:
                     v_copy(step, k, c).wait_send()
                     r_copy(step, k, c).wait_send()
@@ -441,7 +445,7 @@
     each(drain)
     if paired:
         for step in range(2):
-            for c in range(chunks):
+            for c in range(chunks // (step + 1)):
                 for j in range(3):
                     pair_v(step, j, c).wait_send()
                     pair_r(step, j, c).wait_send()

time: 203 us -> 201 us (level)
    pallas_call x1, Pallas kernels: 198 us -> 196 us  [train(): pl.pallas_call(functools.partial(inner_kernel, n, m), out_shape=(pltpu.VM...]
where the time goes in v5:
time: 201 us
  Pallas kernels  196 us (98%)
  local copies, waits for them, and re-layouts  3.95 us (2%)
    pallas_call x1, Pallas kernels, train(): pl.pallas_call(functools.partial(inner_kernel, n, m), out_shape=(pltpu.VM...  196 us

profile of v5, /device:TPU:0, one launch (start us, length us, event | category | flops | bytes accessed | tf_op | source)
XLA Modules:
  0.0 200.6 jit_solution(7310023196888368639)
XLA Ops:
  0.6 196.0 %shard_map.112 = (f32[3072,256]{1,0:T(8,128)S(1)}, f32[3072,128]{1,0:T(8,128)S(1)}, f32[3072,128]{1,0:T(8,128)S(1)}) custom-call(bf16[256,12288]{1,0:T(8,128)(2,1)} %bitcast.9, bf16[256,256]{1,0:T(8,128)(2,1)} %bitcast.14, s32[1,256]{1,0:T(1,128)} %mask.1, f32[1,12288]{1,0:T(1,128)} %bitcast.15, f32[3072,256]{1,0:T(8,128)} %bitcast.10, ...), custom_call_target="tpu_custom_call" | custom-call | flops 6442450944 | bytes 25165824 | tf_op jit(solution)/shard_map/pallas_call | solution.py:464
  196.7 1.7 copy.15
  198.3 1.1 copy.16
  199.5 1.1 copy.17
